TPU v7x, 512 devices: a whole 4x8x8 slice. The times are simulated.
512 devices in a mesh: blk: 128 (over x, z, y_hi, core), aux: 4 (over y_lo).
Axes of the slice: x: 4, y: 8 (y_hi: 2, y_lo: 4; y = y_hi * 4 + y_lo), z: 8, core: 2. Of those that a mesh axis runs over, the one named last changes fastest.
Arguments:
- factors: bfloat16 [2, 3584, 10240], P(None, 'blk', 'aux'), may hold values from -0.0625 to 0.0625
- amplitudes: bfloat16 [8, 3584, 3584], P(None, 'blk'), may hold values from -0.09375 to 0.09375
Outputs:
- ladder: float32 [8, 2, 2], replicated
All inputs are finite; a program needn't handle non-finite values.
Results may differ from a plain program's by a relative error of at most 0.0003.
Values may be sent and summed in bfloat16 or wider, within the bound.
A program may use at most 64 MiB of HBM per device.

v0:
```python
import jax
import jax.numpy as jnp
from jax import lax
from jax.sharding import PartitionSpec as P


def shifted(value, axis, by):
    length = lax.axis_size(axis)
    return lax.ppermute(value, axis, [(i, (i + by) % length) for i in range(length)])


def shards(factors, amplitudes):
    window_rows, block_len, aux_len = factors.shape
    pair_count = amplitudes.shape[0]
    blocks = lax.axis_size("blk")
    device = lax.axis_index("blk")
    count_c, stride_c, stride_d = (8, 1, 8)
    count_d = blocks // count_c
    tiled = amplitudes.reshape(pair_count, block_len, blocks, block_len)

    def piece_for(offset):
        receiver = device + offset
        chosen = (receiver - stride_d * jnp.arange(count_d, dtype=jnp.int32)) % blocks
        return jnp.take(tiled, chosen, axis=2)

    held_factors = [factors]
    held_amps = [piece_for(0)]
    for step in range(1, count_c):
        moved = shifted((factors, piece_for(stride_c * step)), "blk", stride_c * step)
        held_factors.append(moved[0])
        held_amps.append(moved[1])
    window_factors = jnp.stack(held_factors)
    window_amps = jnp.stack(held_amps)

    def tile_sum(total, column_factors, column_index):
        integrals = jnp.einsum(
            "kacq,bdq->kacbd", window_factors, column_factors, preferred_element_type=jnp.float32
        )
        column_amps = lax.dynamic_index_in_dim(
            window_amps, column_index, axis=3, keepdims=False
        ).astype(jnp.float32)
        return total + jnp.einsum(
            "kacbd,kpcd->pab", integrals, column_amps, precision=lax.Precision.HIGHEST
        )

    initial = jnp.zeros((pair_count, window_rows, window_rows), jnp.float32)
    total = tile_sum(initial, factors, 0)

    def advance(step, carry):
        current, running = carry
        current = shifted(current, "blk", stride_d)
        return (current, tile_sum(running, current, step))

    final_pair = lax.fori_loop(1, count_d, advance, (factors, total))
    return lax.psum(final_pair[1], ("blk", "aux"))


def solution(mesh):
    in_specs = (P(None, "blk", "aux"), P(None, "blk", None))
    out_specs = P()
    return jax.shard_map(shards, mesh=mesh, in_specs=in_specs, out_specs=out_specs, check_vma=False)
```

profile of v0, /device:TPU:27, one launch (start us, length us, event | category | flops | bytes accessed | tf_op | source)
XLA Modules:
  0.0 771.9 jit_solution(9556698869711704711)
XLA Ops:
  14.6 20.6 %reshape.8 = bf16[8,28,128,28]{3,2,0,1:T(8,128)(2,1)} reshape(bf16[8,28,3584]{2,0,1:T(8,128)(2,1)} %param.7) | data formatting | bytes 3211264 | tf_op jit(solution)/shard_map/reshape | solution.py:19
  35.1 12.9 %copy.11 = bf16[8,28,128,28]{3,0,2,1:T(8,128)(2,1)} copy(bf16[8,28,128,28]{3,2,0,1:T(8,128)(2,1)} %reshape.8) | data formatting | bytes 3211264 | tf_op jit(solution)/shard_map/reshape | solution.py:19
  53.1 9.5 %collective-permute-start.1 = (bf16[8,28,16,28]{3,0,1,2:T(8,128)(2,1)}, bf16[8,28,16,28]{3,0,1,2:T(8,128)(2,1)}, u32[]{:S(2)}, u32[]{:S(2)}) collective-permute-start(bf16[8,28,16,28]{3,0,1,2:T(8,128)(2,1)} %select_bitcast_fusion.6), channel_id=1, source_target_pairs={{0,4},{4,8},{8,12},{12,16},{16,20},{20,24},{24,28},{28,32},{32,36}... | collective-permute-start | bytes 602120 | tf_op jit(solution)/shard_map/ppermute | solution.py:9
  106.2 41.6 %collective-permute-done.2 = bf16[8,28,16,28]{3,0,1,2:T(8,128)(2,1)S(1)} collective-permute-done((bf16[8,28,16,28]{3,0,1,2:T(8,128)(2,1)S(1)}, bf16[8,28,16,28]{3,0,1,2:T(8,128)(2,1)S(1)}, u32[]{:S(2)}, u32[]{:S(2)}) %collective-permute-start.2) | collective-permute-done | bytes 200736 | tf_op jit(solution)/shard_map/ppermute | solution.py:9
  150.1 12.9 %collective-permute-done.3 = bf16[8,28,16,28]{3,0,1,2:T(8,128)(2,1)S(1)} collective-permute-done((bf16[8,28,16,28]{3,0,1,2:T(8,128)(2,1)S(1)}, bf16[8,28,16,28]{3,0,1,2:T(8,128)(2,1)S(1)}, u32[]{:S(2)}, u32[]{:S(2)}) %collective-permute-start.3) | collective-permute-done | bytes 200736 | tf_op jit(solution)/shard_map/ppermute | solution.py:9
  165.6 41.9 %collective-permute-done.4 = bf16[8,28,16,28]{3,0,1,2:T(8,128)(2,1)S(1)} collective-permute-done((bf16[8,28,16,28]{3,0,1,2:T(8,128)(2,1)S(1)}, bf16[8,28,16,28]{3,0,1,2:T(8,128)(2,1)S(1)}, u32[]{:S(2)}, u32[]{:S(2)}) %collective-permute-start.4) | collective-permute-done | bytes 200736 | tf_op jit(solution)/shard_map/ppermute | solution.py:9
  209.8 16.0 %collective-permute-done.5 = bf16[8,28,16,28]{3,0,1,2:T(8,128)(2,1)S(1)} collective-permute-done((bf16[8,28,16,28]{3,0,1,2:T(8,128)(2,1)S(1)}, bf16[8,28,16,28]{3,0,1,2:T(8,128)(2,1)S(1)}, u32[]{:S(2)}, u32[]{:S(2)}) %collective-permute-start.5) | collective-permute-done | bytes 200736 | tf_op jit(solution)/shard_map/ppermute | solution.py:9
  228.0 30.0 %collective-permute-done.6 = bf16[8,28,16,28]{3,0,1,2:T(8,128)(2,1)S(1)} collective-permute-done((bf16[8,28,16,28]{3,0,1,2:T(8,128)(2,1)S(1)}, bf16[8,28,16,28]{3,0,1,2:T(8,128)(2,1)S(1)}, u32[]{:S(2)}, u32[]{:S(2)}) %collective-permute-start.6) | collective-permute-done | bytes 200736 | tf_op jit(solution)/shard_map/ppermute | solution.py:9
  262.4 25.8 %collective-permute-done.7 = bf16[8,28,16,28]{3,0,1,2:T(8,128)(2,1)S(1)} collective-permute-done((bf16[8,28,16,28]{3,0,1,2:T(8,128)(2,1)S(1)}, bf16[8,28,16,28]{3,0,1,2:T(8,128)(2,1)S(1)}, u32[]{:S(2)}, u32[]{:S(2)}) %collective-permute-start.7) | collective-permute-done | bytes 200736 | tf_op jit(solution)/shard_map/ppermute | solution.py:9
  291.6 20.3 %collective-permute-start.13 = (bf16[2,28,2560]{2,1,0:T(8,128)(2,1)S(1)}, bf16[2,28,2560]{2,1,0:T(8,128)(2,1)S(1)}, u32[]{:S(2)}, u32[]{:S(2)}) collective-permute-start(bf16[2,28,2560]{2,1,0:T(8,128)(2,1)S(1)} %copy.19), channel_id=1, source_target_pairs={{0,24},{4,28},{8,32},{12,36},{16,40},{20,44},{24,48},{28,52},{32,5... | collective-permute-start | bytes 860168 | tf_op jit(solution)/shard_map/ppermute | solution.py:9
  316.0 13.3 %collective-permute-done.13 = bf16[2,28,2560]{2,1,0:T(8,128)(2,1)S(1)} collective-permute-done((bf16[2,28,2560]{2,1,0:T(8,128)(2,1)S(1)}, bf16[2,28,2560]{2,1,0:T(8,128)(2,1)S(1)}, u32[]{:S(2)}, u32[]{:S(2)}) %collective-permute-start.13) | collective-permute-done | bytes 286752 | tf_op jit(solution)/shard_map/ppermute | solution.py:9
  329.3 10.3 %collective-permute-done.14 = bf16[2,28,2560]{2,1,0:T(8,128)(2,1)S(1)} collective-permute-done((bf16[2,28,2560]{2,1,0:T(8,128)(2,1)S(1)}, bf16[2,28,2560]{2,1,0:T(8,128)(2,1)S(1)}, u32[]{:S(2)}, u32[]{:S(2)}) %collective-permute-start.14) | collective-permute-done | bytes 286752 | tf_op jit(solution)/shard_map/ppermute | solution.py:9
  341.9 301.9 %while.17 = (s32[]{:T(128)}, bf16[2,28,2560]{2,0,1:T(2,128)(2,1)S(1)}, f32[8,2,2]{0,2,1:T(2,128)S(1)}, bf16[8,8,28,16,28]{4,1,0,2,3:T(8,128)(2,1)}, bf16[8,2,28,...) while((s32[]{:T(128)}, bf16[2,28,2560]{2,0,1:T(2,128)(2,1)S(1)}, ...), condition=%wide.region_1.3_spmd, body=%wide.region_0.2_spmd.sunk | while | flops 130859040 | bytes 4960683 | solution.py:54
  341.9 16.3 %collective-permute-start = (bf16[2,28,2560]{2,0,1:T(2,128)(2,1)S(1)}, bf16[2,28,2560]{2,0,1:T(2,128)(2,1)S(1)}, u32[]{:S(2)}, u32[]{:S(2)}) collective-permute-start(bf16[2,28,2560]{2,0,1:T(2,128)(2,1)S(1)} %get-tuple-element.195), channel_id=1, source_target_pairs={{0,32},{4,36},{8,40},{12,44},{16,48},{20,52},{24,56},{28,60},{32,6... | collective-permute-start | bytes 860168 | tf_op jit(solution)/shard_map/while/body/eval_jaxpr/ppermute | solution.py:9
  358.2 6.6 collective-permute-done
  373.1 12.9 %collective-permute-done = bf16[2,28,2560]{2,0,1:T(2,128)(2,1)S(1)} collective-permute-done((bf16[2,28,2560]{2,0,1:T(2,128)(2,1)S(1)}, bf16[2,28,2560]{2,0,1:T(2,128)(2,1)S(1)}, u32[]{:S(2)}, u32[]{:S(2)}) %collective-permute-start) | collective-permute-done | bytes 286752 | tf_op jit(solution)/shard_map/while/body/eval_jaxpr/ppermute | solution.py:9
  391.7 11.6 %collective-permute-done = bf16[2,28,2560]{2,0,1:T(2,128)(2,1)S(1)} collective-permute-done((bf16[2,28,2560]{2,0,1:T(2,128)(2,1)S(1)}, bf16[2,28,2560]{2,0,1:T(2,128)(2,1)S(1)}, u32[]{:S(2)}, u32[]{:S(2)}) %collective-permute-start) | collective-permute-done | bytes 286752 | tf_op jit(solution)/shard_map/while/body/eval_jaxpr/ppermute | solution.py:9
  408.9 11.0 %collective-permute-done = bf16[2,28,2560]{2,0,1:T(2,128)(2,1)S(1)} collective-permute-done((bf16[2,28,2560]{2,0,1:T(2,128)(2,1)S(1)}, bf16[2,28,2560]{2,0,1:T(2,128)(2,1)S(1)}, u32[]{:S(2)}, u32[]{:S(2)}) %collective-permute-start) | collective-permute-done | bytes 286752 | tf_op jit(solution)/shard_map/while/body/eval_jaxpr/ppermute | solution.py:9
  425.4 8.5 %collective-permute-done = bf16[2,28,2560]{2,0,1:T(2,128)(2,1)S(1)} collective-permute-done((bf16[2,28,2560]{2,0,1:T(2,128)(2,1)S(1)}, bf16[2,28,2560]{2,0,1:T(2,128)(2,1)S(1)}, u32[]{:S(2)}, u32[]{:S(2)}) %collective-permute-start) | collective-permute-done | bytes 286752 | tf_op jit(solution)/shard_map/while/body/eval_jaxpr/ppermute | solution.py:9
  439.4 11.2 %collective-permute-done = bf16[2,28,2560]{2,0,1:T(2,128)(2,1)S(1)} collective-permute-done((bf16[2,28,2560]{2,0,1:T(2,128)(2,1)S(1)}, bf16[2,28,2560]{2,0,1:T(2,128)(2,1)S(1)}, u32[]{:S(2)}, u32[]{:S(2)}) %collective-permute-start) | collective-permute-done | bytes 286752 | tf_op jit(solution)/shard_map/while/body/eval_jaxpr/ppermute | solution.py:9
  454.2 8.8 %collective-permute-start = (bf16[2,28,2560]{2,0,1:T(2,128)(2,1)S(1)}, bf16[2,28,2560]{2,0,1:T(2,128)(2,1)S(1)}, u32[]{:S(2)}, u32[]{:S(2)}) collective-permute-start(bf16[2,28,2560]{2,0,1:T(2,128)(2,1)S(1)} %get-tuple-element.195), channel_id=1, source_target_pairs={{0,32},{4,36},{8,40},{12,44},{16,48},{20,52},{24,56},{28,60},{32,6... | collective-permute-start | bytes 860168 | tf_op jit(solution)/shard_map/while/body/eval_jaxpr/ppermute | solution.py:9
  470.5 10.5 %collective-permute-start = (bf16[2,28,2560]{2,0,1:T(2,128)(2,1)S(1)}, bf16[2,28,2560]{2,0,1:T(2,128)(2,1)S(1)}, u32[]{:S(2)}, u32[]{:S(2)}) collective-permute-start(bf16[2,28,2560]{2,0,1:T(2,128)(2,1)S(1)} %get-tuple-element.195), channel_id=1, source_target_pairs={{0,32},{4,36},{8,40},{12,44},{16,48},{20,52},{24,56},{28,60},{32,6... | collective-permute-start | bytes 860168 | tf_op jit(solution)/shard_map/while/body/eval_jaxpr/ppermute | solution.py:9
  490.8 21.1 %collective-permute-start = (bf16[2,28,2560]{2,0,1:T(2,128)(2,1)S(1)}, bf16[2,28,2560]{2,0,1:T(2,128)(2,1)S(1)}, u32[]{:S(2)}, u32[]{:S(2)}) collective-permute-start(bf16[2,28,2560]{2,0,1:T(2,128)(2,1)S(1)} %get-tuple-element.195), channel_id=1, source_target_pairs={{0,32},{4,36},{8,40},{12,44},{16,48},{20,52},{24,56},{28,60},{32,6... | collective-permute-start | bytes 860168 | tf_op jit(solution)/shard_map/while/body/eval_jaxpr/ppermute | solution.py:9
  512.0 8.4 %collective-permute-done = bf16[2,28,2560]{2,0,1:T(2,128)(2,1)S(1)} collective-permute-done((bf16[2,28,2560]{2,0,1:T(2,128)(2,1)S(1)}, bf16[2,28,2560]{2,0,1:T(2,128)(2,1)S(1)}, u32[]{:S(2)}, u32[]{:S(2)}) %collective-permute-start) | collective-permute-done | bytes 286752 | tf_op jit(solution)/shard_map/while/body/eval_jaxpr/ppermute | solution.py:9
  529.1 7.7 %collective-permute-done = bf16[2,28,2560]{2,0,1:T(2,128)(2,1)S(1)} collective-permute-done((bf16[2,28,2560]{2,0,1:T(2,128)(2,1)S(1)}, bf16[2,28,2560]{2,0,1:T(2,128)(2,1)S(1)}, u32[]{:S(2)}, u32[]{:S(2)}) %collective-permute-start) | collective-permute-done | bytes 286752 | tf_op jit(solution)/shard_map/while/body/eval_jaxpr/ppermute | solution.py:9
  540.5 17.4 %collective-permute-start = (bf16[2,28,2560]{2,0,1:T(2,128)(2,1)S(1)}, bf16[2,28,2560]{2,0,1:T(2,128)(2,1)S(1)}, u32[]{:S(2)}, u32[]{:S(2)}) collective-permute-start(bf16[2,28,2560]{2,0,1:T(2,128)(2,1)S(1)} %get-tuple-element.195), channel_id=1, source_target_pairs={{0,32},{4,36},{8,40},{12,44},{16,48},{20,52},{24,56},{28,60},{32,6... | collective-permute-start | bytes 860168 | tf_op jit(solution)/shard_map/while/body/eval_jaxpr/ppermute | solution.py:9
  557.9 9.5 %collective-permute-done = bf16[2,28,2560]{2,0,1:T(2,128)(2,1)S(1)} collective-permute-done((bf16[2,28,2560]{2,0,1:T(2,128)(2,1)S(1)}, bf16[2,28,2560]{2,0,1:T(2,128)(2,1)S(1)}, u32[]{:S(2)}, u32[]{:S(2)}) %collective-permute-start) | collective-permute-done | bytes 286752 | tf_op jit(solution)/shard_map/while/body/eval_jaxpr/ppermute | solution.py:9
  576.1 8.1 %collective-permute-done = bf16[2,28,2560]{2,0,1:T(2,128)(2,1)S(1)} collective-permute-done((bf16[2,28,2560]{2,0,1:T(2,128)(2,1)S(1)}, bf16[2,28,2560]{2,0,1:T(2,128)(2,1)S(1)}, u32[]{:S(2)}, u32[]{:S(2)}) %collective-permute-start) | collective-permute-done | bytes 286752 | tf_op jit(solution)/shard_map/while/body/eval_jaxpr/ppermute | solution.py:9
  592.8 11.2 %collective-permute-done = bf16[2,28,2560]{2,0,1:T(2,128)(2,1)S(1)} collective-permute-done((bf16[2,28,2560]{2,0,1:T(2,128)(2,1)S(1)}, bf16[2,28,2560]{2,0,1:T(2,128)(2,1)S(1)}, u32[]{:S(2)}, u32[]{:S(2)}) %collective-permute-start) | collective-permute-done | bytes 286752 | tf_op jit(solution)/shard_map/while/body/eval_jaxpr/ppermute | solution.py:9
  612.7 12.3 %collective-permute-done = bf16[2,28,2560]{2,0,1:T(2,128)(2,1)S(1)} collective-permute-done((bf16[2,28,2560]{2,0,1:T(2,128)(2,1)S(1)}, bf16[2,28,2560]{2,0,1:T(2,128)(2,1)S(1)}, u32[]{:S(2)}, u32[]{:S(2)}) %collective-permute-start) | collective-permute-done | bytes 286752 | tf_op jit(solution)/shard_map/while/body/eval_jaxpr/ppermute | solution.py:9
  630.6 9.6 %collective-permute-done = bf16[2,28,2560]{2,0,1:T(2,128)(2,1)S(1)} collective-permute-done((bf16[2,28,2560]{2,0,1:T(2,128)(2,1)S(1)}, bf16[2,28,2560]{2,0,1:T(2,128)(2,1)S(1)}, u32[]{:S(2)}, u32[]{:S(2)}) %collective-permute-start) | collective-permute-done | bytes 286752 | tf_op jit(solution)/shard_map/while/body/eval_jaxpr/ppermute | solution.py:9
  643.8 128.1 %psum.7 = f32[8,2,2]{0,2,1:T(2,128)} all-reduce(f32[8,2,2]{0,2,1:T(2,128)S(1)} %get-tuple-element.138), channel_id=1, replica_groups=mesh['blk'=128,'aux'=4] {'blk','aux'}, use_global_device_ids=true, to_apply=%region_2.4 | all-reduce | flops 32 | bytes 256 | tf_op jit(solution)/shard_map/psum | solution.py:55
  (141 shorter events, 184.8 us)
Async XLA Ops:
  1.0 289.4 %collective-permute-start.8 = (bf16[2,28,2560]{2,1,0:T(8,128)(2,1)S(1)}, bf16[2,28,2560]{2,1,0:T(8,128)(2,1)}, u32[]{:S(2)}, u32[]{:S(2)}) collective-permute-start(bf16[2,28,2560]{2,1,0:T(8,128)(2,1)S(1)} %copy.19), channel_id=1, source_target_pairs={{0,4},{4,8},{8,12},{12,16},{16,20},{20,24},{24,28},{28,32},{32,36}... | collective-permute-start | bytes 860168 | tf_op jit(solution)/shard_map/ppermute | solution.py:9
  6.3 305.6 %collective-permute-start.9 = (bf16[2,28,2560]{2,1,0:T(8,128)(2,1)S(1)}, bf16[2,28,2560]{2,1,0:T(8,128)(2,1)}, u32[]{:S(2)}, u32[]{:S(2)}) collective-permute-start(bf16[2,28,2560]{2,1,0:T(8,128)(2,1)S(1)} %copy.19), channel_id=1, source_target_pairs={{0,8},{4,12},{8,16},{12,20},{16,24},{20,28},{24,32},{28,36},{32,40... | collective-permute-start | bytes 860168 | tf_op jit(solution)/shard_map/ppermute | solution.py:9
  12.6 302.3 %collective-permute-start.10 = (bf16[2,28,2560]{2,1,0:T(8,128)(2,1)S(1)}, bf16[2,28,2560]{2,1,0:T(8,128)(2,1)}, u32[]{:S(2)}, u32[]{:S(2)}) collective-permute-start(bf16[2,28,2560]{2,1,0:T(8,128)(2,1)S(1)} %copy.19), channel_id=1, source_target_pairs={{0,12},{4,16},{8,20},{12,24},{16,28},{20,32},{24,36},{28,40},{32,4... | collective-permute-start | bytes 860168 | tf_op jit(solution)/shard_map/ppermute | solution.py:9
  53.1 49.6 %collective-permute-start.1 = (bf16[8,28,16,28]{3,0,1,2:T(8,128)(2,1)}, bf16[8,28,16,28]{3,0,1,2:T(8,128)(2,1)}, u32[]{:S(2)}, u32[]{:S(2)}) collective-permute-start(bf16[8,28,16,28]{3,0,1,2:T(8,128)(2,1)} %select_bitcast_fusion.6), channel_id=1, source_target_pairs={{0,4},{4,8},{8,12},{12,16},{16,20},{20,24},{24,28},{28,32},{32,36}... | collective-permute-start | bytes 602120 | tf_op jit(solution)/shard_map/ppermute | solution.py:9
  95.2 2.5 copy-start.2
  97.7 192.7 %copy-start.4 = (bf16[8,2,28,2560]{3,2,1,0:T(8,128)(2,1)S(1)}, bf16[8,2,28,2560]{3,2,1,0:T(8,128)(2,1)}, u32[]{:S(2)}) copy-start(bf16[8,2,28,2560]{3,2,1,0:T(8,128)(2,1)} %bitcast_dynamic-update-slice_fusion.15) | copy-start | bytes 6881284
  97.8 50.0 %collective-permute-start.2 = (bf16[8,28,16,28]{3,0,1,2:T(8,128)(2,1)S(1)}, bf16[8,28,16,28]{3,0,1,2:T(8,128)(2,1)S(1)}, u32[]{:S(2)}, u32[]{:S(2)}) collective-permute-start(bf16[8,28,16,28]{3,0,1,2:T(8,128)(2,1)S(1)} %select_bitcast_fusion.5), channel_id=1, source_target_pairs={{0,8},{4,12},{8,16},{12,20},{16,24},{20,28},{24,32},{28,36},{32,40... | collective-permute-start | bytes 602120 | tf_op jit(solution)/shard_map/ppermute | solution.py:9
  104.2 58.8 %collective-permute-start.3 = (bf16[8,28,16,28]{3,0,1,2:T(8,128)(2,1)S(1)}, bf16[8,28,16,28]{3,0,1,2:T(8,128)(2,1)S(1)}, u32[]{:S(2)}, u32[]{:S(2)}) collective-permute-start(bf16[8,28,16,28]{3,0,1,2:T(8,128)(2,1)S(1)} %select_bitcast_fusion.4), channel_id=1, source_target_pairs={{0,12},{4,16},{8,20},{12,24},{16,28},{20,32},{24,36},{28,40},{32,4... | collective-permute-start | bytes 602120 | tf_op jit(solution)/shard_map/ppermute | solution.py:9
  148.1 59.4 %collective-permute-start.4 = (bf16[8,28,16,28]{3,0,1,2:T(8,128)(2,1)S(1)}, bf16[8,28,16,28]{3,0,1,2:T(8,128)(2,1)S(1)}, u32[]{:S(2)}, u32[]{:S(2)}) collective-permute-start(bf16[8,28,16,28]{3,0,1,2:T(8,128)(2,1)S(1)} %select_bitcast_fusion.3), channel_id=1, source_target_pairs={{0,16},{4,20},{8,24},{12,28},{16,32},{20,36},{24,40},{28,44},{32,4... | collective-permute-start | bytes 602120 | tf_op jit(solution)/shard_map/ppermute | solution.py:9
  163.3 62.4 %collective-permute-start.5 = (bf16[8,28,16,28]{3,0,1,2:T(8,128)(2,1)S(1)}, bf16[8,28,16,28]{3,0,1,2:T(8,128)(2,1)S(1)}, u32[]{:S(2)}, u32[]{:S(2)}) collective-permute-start(bf16[8,28,16,28]{3,0,1,2:T(8,128)(2,1)S(1)} %select_bitcast_fusion.2), channel_id=1, source_target_pairs={{0,20},{4,24},{8,28},{12,32},{16,36},{20,40},{24,44},{28,48},{32,5... | collective-permute-start | bytes 602120 | tf_op jit(solution)/shard_map/ppermute | solution.py:9
  207.8 50.1 %collective-permute-start.6 = (bf16[8,28,16,28]{3,0,1,2:T(8,128)(2,1)S(1)}, bf16[8,28,16,28]{3,0,1,2:T(8,128)(2,1)S(1)}, u32[]{:S(2)}, u32[]{:S(2)}) collective-permute-start(bf16[8,28,16,28]{3,0,1,2:T(8,128)(2,1)S(1)} %select_bitcast_fusion.1), channel_id=1, source_target_pairs={{0,24},{4,28},{8,32},{12,36},{16,40},{20,44},{24,48},{28,52},{32,5... | collective-permute-start | bytes 602120 | tf_op jit(solution)/shard_map/ppermute | solution.py:9
  226.1 62.1 %collective-permute-start.7 = (bf16[8,28,16,28]{3,0,1,2:T(8,128)(2,1)S(1)}, bf16[8,28,16,28]{3,0,1,2:T(8,128)(2,1)S(1)}, u32[]{:S(2)}, u32[]{:S(2)}) collective-permute-start(bf16[8,28,16,28]{3,0,1,2:T(8,128)(2,1)S(1)} %select_bitcast_fusion), channel_id=1, source_target_pairs={{0,28},{4,32},{8,36},{12,40},{16,44},{20,48},{24,52},{28,56},{32,6... | collective-permute-start | bytes 602120 | tf_op jit(solution)/shard_map/ppermute | solution.py:9
  258.3 57.7 %collective-permute-start.11 = (bf16[2,28,2560]{2,1,0:T(8,128)(2,1)S(1)}, bf16[2,28,2560]{2,1,0:T(8,128)(2,1)S(1)}, u32[]{:S(2)}, u32[]{:S(2)}) collective-permute-start(bf16[2,28,2560]{2,1,0:T(8,128)(2,1)S(1)} %copy.19), channel_id=1, source_target_pairs={{0,16},{4,20},{8,24},{12,28},{16,32},{20,36},{24,40},{28,44},{32,4... | collective-permute-start | bytes 860168 | tf_op jit(solution)/shard_map/ppermute | solution.py:9
  288.4 53.4 %copy-start.3 = (bf16[8,8,28,16,28]{4,1,0,2,3:T(8,128)(2,1)}, bf16[8,8,28,16,28]{4,1,0,2,3:T(8,128)(2,1)S(1)}, u32[]{:S(2)}) copy-start(bf16[8,8,28,16,28]{4,1,0,2,3:T(8,128)(2,1)S(1)} %bitcast_dynamic-update-slice_fusion.1) | copy-start | bytes 4816900
  288.4 27.5 %collective-permute-start.12 = (bf16[2,28,2560]{2,1,0:T(8,128)(2,1)S(1)}, bf16[2,28,2560]{2,1,0:T(8,128)(2,1)S(1)}, u32[]{:S(2)}, u32[]{:S(2)}) collective-permute-start(bf16[2,28,2560]{2,1,0:T(8,128)(2,1)S(1)} %copy.19), channel_id=1, source_target_pairs={{0,20},{4,24},{8,28},{12,32},{16,36},{20,40},{24,44},{28,48},{32,5... | collective-permute-start | bytes 860168 | tf_op jit(solution)/shard_map/ppermute | solution.py:9
  291.6 37.7 %collective-permute-start.13 = (bf16[2,28,2560]{2,1,0:T(8,128)(2,1)S(1)}, bf16[2,28,2560]{2,1,0:T(8,128)(2,1)S(1)}, u32[]{:S(2)}, u32[]{:S(2)}) collective-permute-start(bf16[2,28,2560]{2,1,0:T(8,128)(2,1)S(1)} %copy.19), channel_id=1, source_target_pairs={{0,24},{4,28},{8,32},{12,36},{16,40},{20,44},{24,48},{28,52},{32,5... | collective-permute-start | bytes 860168 | tf_op jit(solution)/shard_map/ppermute | solution.py:9
  313.0 26.6 %collective-permute-start.14 = (bf16[2,28,2560]{2,1,0:T(8,128)(2,1)S(1)}, bf16[2,28,2560]{2,1,0:T(8,128)(2,1)S(1)}, u32[]{:S(2)}, u32[]{:S(2)}) collective-permute-start(bf16[2,28,2560]{2,1,0:T(8,128)(2,1)S(1)} %copy.19), channel_id=1, source_target_pairs={{0,28},{4,32},{8,36},{12,40},{16,44},{20,48},{24,52},{28,56},{32,6... | collective-permute-start | bytes 860168 | tf_op jit(solution)/shard_map/ppermute | solution.py:9
  341.9 22.9 %collective-permute-start = (bf16[2,28,2560]{2,0,1:T(2,128)(2,1)S(1)}, bf16[2,28,2560]{2,0,1:T(2,128)(2,1)S(1)}, u32[]{:S(2)}, u32[]{:S(2)}) collective-permute-start(bf16[2,28,2560]{2,0,1:T(2,128)(2,1)S(1)} %get-tuple-element.195), channel_id=1, source_target_pairs={{0,32},{4,36},{8,40},{12,44},{16,48},{20,52},{24,56},{28,60},{32,6... | collective-permute-start | bytes 860168 | tf_op jit(solution)/shard_map/while/body/eval_jaxpr/ppermute | solution.py:9
  368.4 17.6 %collective-permute-start = (bf16[2,28,2560]{2,0,1:T(2,128)(2,1)S(1)}, bf16[2,28,2560]{2,0,1:T(2,128)(2,1)S(1)}, u32[]{:S(2)}, u32[]{:S(2)}) collective-permute-start(bf16[2,28,2560]{2,0,1:T(2,128)(2,1)S(1)} %get-tuple-element.195), channel_id=1, source_target_pairs={{0,32},{4,36},{8,40},{12,44},{16,48},{20,52},{24,56},{28,60},{32,6... | collective-permute-start | bytes 860168 | tf_op jit(solution)/shard_map/while/body/eval_jaxpr/ppermute | solution.py:9
  389.7 13.6 %collective-permute-start = (bf16[2,28,2560]{2,0,1:T(2,128)(2,1)S(1)}, bf16[2,28,2560]{2,0,1:T(2,128)(2,1)S(1)}, u32[]{:S(2)}, u32[]{:S(2)}) collective-permute-start(bf16[2,28,2560]{2,0,1:T(2,128)(2,1)S(1)} %get-tuple-element.195), channel_id=1, source_target_pairs={{0,32},{4,36},{8,40},{12,44},{16,48},{20,52},{24,56},{28,60},{32,6... | collective-permute-start | bytes 860168 | tf_op jit(solution)/shard_map/while/body/eval_jaxpr/ppermute | solution.py:9
  406.9 12.9 %collective-permute-start = (bf16[2,28,2560]{2,0,1:T(2,128)(2,1)S(1)}, bf16[2,28,2560]{2,0,1:T(2,128)(2,1)S(1)}, u32[]{:S(2)}, u32[]{:S(2)}) collective-permute-start(bf16[2,28,2560]{2,0,1:T(2,128)(2,1)S(1)} %get-tuple-element.195), channel_id=1, source_target_pairs={{0,32},{4,36},{8,40},{12,44},{16,48},{20,52},{24,56},{28,60},{32,6... | collective-permute-start | bytes 860168 | tf_op jit(solution)/shard_map/while/body/eval_jaxpr/ppermute | solution.py:9
  423.5 10.4 %collective-permute-start = (bf16[2,28,2560]{2,0,1:T(2,128)(2,1)S(1)}, bf16[2,28,2560]{2,0,1:T(2,128)(2,1)S(1)}, u32[]{:S(2)}, u32[]{:S(2)}) collective-permute-start(bf16[2,28,2560]{2,0,1:T(2,128)(2,1)S(1)} %get-tuple-element.195), channel_id=1, source_target_pairs={{0,32},{4,36},{8,40},{12,44},{16,48},{20,52},{24,56},{28,60},{32,6... | collective-permute-start | bytes 860168 | tf_op jit(solution)/shard_map/while/body/eval_jaxpr/ppermute | solution.py:9
  437.5 13.1 %collective-permute-start = (bf16[2,28,2560]{2,0,1:T(2,128)(2,1)S(1)}, bf16[2,28,2560]{2,0,1:T(2,128)(2,1)S(1)}, u32[]{:S(2)}, u32[]{:S(2)}) collective-permute-start(bf16[2,28,2560]{2,0,1:T(2,128)(2,1)S(1)} %get-tuple-element.195), channel_id=1, source_target_pairs={{0,32},{4,36},{8,40},{12,44},{16,48},{20,52},{24,56},{28,60},{32,6... | collective-permute-start | bytes 860168 | tf_op jit(solution)/shard_map/while/body/eval_jaxpr/ppermute | solution.py:9
  454.2 12.7 %collective-permute-start = (bf16[2,28,2560]{2,0,1:T(2,128)(2,1)S(1)}, bf16[2,28,2560]{2,0,1:T(2,128)(2,1)S(1)}, u32[]{:S(2)}, u32[]{:S(2)}) collective-permute-start(bf16[2,28,2560]{2,0,1:T(2,128)(2,1)S(1)} %get-tuple-element.195), channel_id=1, source_target_pairs={{0,32},{4,36},{8,40},{12,44},{16,48},{20,52},{24,56},{28,60},{32,6... | collective-permute-start | bytes 860168 | tf_op jit(solution)/shard_map/while/body/eval_jaxpr/ppermute | solution.py:9
  470.5 16.7 %collective-permute-start = (bf16[2,28,2560]{2,0,1:T(2,128)(2,1)S(1)}, bf16[2,28,2560]{2,0,1:T(2,128)(2,1)S(1)}, u32[]{:S(2)}, u32[]{:S(2)}) collective-permute-start(bf16[2,28,2560]{2,0,1:T(2,128)(2,1)S(1)} %get-tuple-element.195), channel_id=1, source_target_pairs={{0,32},{4,36},{8,40},{12,44},{16,48},{20,52},{24,56},{28,60},{32,6... | collective-permute-start | bytes 860168 | tf_op jit(solution)/shard_map/while/body/eval_jaxpr/ppermute | solution.py:9
  490.8 29.6 %collective-permute-start = (bf16[2,28,2560]{2,0,1:T(2,128)(2,1)S(1)}, bf16[2,28,2560]{2,0,1:T(2,128)(2,1)S(1)}, u32[]{:S(2)}, u32[]{:S(2)}) collective-permute-start(bf16[2,28,2560]{2,0,1:T(2,128)(2,1)S(1)} %get-tuple-element.195), channel_id=1, source_target_pairs={{0,32},{4,36},{8,40},{12,44},{16,48},{20,52},{24,56},{28,60},{32,6... | collective-permute-start | bytes 860168 | tf_op jit(solution)/shard_map/while/body/eval_jaxpr/ppermute | solution.py:9
  524.1 12.8 %collective-permute-start = (bf16[2,28,2560]{2,0,1:T(2,128)(2,1)S(1)}, bf16[2,28,2560]{2,0,1:T(2,128)(2,1)S(1)}, u32[]{:S(2)}, u32[]{:S(2)}) collective-permute-start(bf16[2,28,2560]{2,0,1:T(2,128)(2,1)S(1)} %get-tuple-element.195), channel_id=1, source_target_pairs={{0,32},{4,36},{8,40},{12,44},{16,48},{20,52},{24,56},{28,60},{32,6... | collective-permute-start | bytes 860168 | tf_op jit(solution)/shard_map/while/body/eval_jaxpr/ppermute | solution.py:9
  540.5 27.0 %collective-permute-start = (bf16[2,28,2560]{2,0,1:T(2,128)(2,1)S(1)}, bf16[2,28,2560]{2,0,1:T(2,128)(2,1)S(1)}, u32[]{:S(2)}, u32[]{:S(2)}) collective-permute-start(bf16[2,28,2560]{2,0,1:T(2,128)(2,1)S(1)} %get-tuple-element.195), channel_id=1, source_target_pairs={{0,32},{4,36},{8,40},{12,44},{16,48},{20,52},{24,56},{28,60},{32,6... | collective-permute-start | bytes 860168 | tf_op jit(solution)/shard_map/while/body/eval_jaxpr/ppermute | solution.py:9
  571.1 13.1 %collective-permute-start = (bf16[2,28,2560]{2,0,1:T(2,128)(2,1)S(1)}, bf16[2,28,2560]{2,0,1:T(2,128)(2,1)S(1)}, u32[]{:S(2)}, u32[]{:S(2)}) collective-permute-start(bf16[2,28,2560]{2,0,1:T(2,128)(2,1)S(1)} %get-tuple-element.195), channel_id=1, source_target_pairs={{0,32},{4,36},{8,40},{12,44},{16,48},{20,52},{24,56},{28,60},{32,6... | collective-permute-start | bytes 860168 | tf_op jit(solution)/shard_map/while/body/eval_jaxpr/ppermute | solution.py:9
  587.8 16.3 %collective-permute-start = (bf16[2,28,2560]{2,0,1:T(2,128)(2,1)S(1)}, bf16[2,28,2560]{2,0,1:T(2,128)(2,1)S(1)}, u32[]{:S(2)}, u32[]{:S(2)}) collective-permute-start(bf16[2,28,2560]{2,0,1:T(2,128)(2,1)S(1)} %get-tuple-element.195), channel_id=1, source_target_pairs={{0,32},{4,36},{8,40},{12,44},{16,48},{20,52},{24,56},{28,60},{32,6... | collective-permute-start | bytes 860168 | tf_op jit(solution)/shard_map/while/body/eval_jaxpr/ppermute | solution.py:9
  607.7 17.3 %collective-permute-start = (bf16[2,28,2560]{2,0,1:T(2,128)(2,1)S(1)}, bf16[2,28,2560]{2,0,1:T(2,128)(2,1)S(1)}, u32[]{:S(2)}, u32[]{:S(2)}) collective-permute-start(bf16[2,28,2560]{2,0,1:T(2,128)(2,1)S(1)} %get-tuple-element.195), channel_id=1, source_target_pairs={{0,32},{4,36},{8,40},{12,44},{16,48},{20,52},{24,56},{28,60},{32,6... | collective-permute-start | bytes 860168 | tf_op jit(solution)/shard_map/while/body/eval_jaxpr/ppermute | solution.py:9
  628.6 11.5 %collective-permute-start = (bf16[2,28,2560]{2,0,1:T(2,128)(2,1)S(1)}, bf16[2,28,2560]{2,0,1:T(2,128)(2,1)S(1)}, u32[]{:S(2)}, u32[]{:S(2)}) collective-permute-start(bf16[2,28,2560]{2,0,1:T(2,128)(2,1)S(1)} %get-tuple-element.195), channel_id=1, source_target_pairs={{0,32},{4,36},{8,40},{12,44},{16,48},{20,52},{24,56},{28,60},{32,6... | collective-permute-start | bytes 860168 | tf_op jit(solution)/shard_map/while/body/eval_jaxpr/ppermute | solution.py:9
  (2 other events, 4.5 us)
where the time goes:
time: 774 us; the launch traced here: 772 us
  waiting for transfers between devices  330 us (43%)
  starting transfers between devices  175 us (23%)
  blocking collectives  128 us (17%)
  local copies, waits for them, and re-layouts  80.3 us (10%)
  matrix products  53.2 us (7%)
    ppermute x29, waiting for transfers between devices, shifted(): lax.ppermute(value, axis, [(i, (i + by) % length) for i in range(length)])  330 us
    ppermute x29, starting transfers between devices, shifted(): lax.ppermute(value, axis, [(i, (i + by) % length) for i in range(length)])  175 us
    psum x1, blocking collectives, shards(): return lax.psum(final_pair[1], ('blk', 'aux'))  128 us
    dot_general x16, matrix products, tile_sum(): jnp.einsum('kacbd,kpcd->pab', integrals, column_amps, precision=lax.Preci...  39.6 us
    gather x8, local copies, waits for them, and re-layouts, piece_for(): return jnp.take(tiled, chosen, axis=2)  35.4 us
    reshape x2, local copies, waits for them, and re-layouts, shards(): tiled = amplitudes.reshape(pair_count, block_len, blocks, block_len)  33.4 us
  transfers between devices with their start and end apart: 29, of which 23 were waited for; matrix products, arithmetic and copies ran while one was open for 10% of the time, Pallas kernels for 0%

commit v1 on v0

v1 whole, which is shorter than its diff:
```python
import jax
import jax.numpy as jnp
from jax import lax
from jax.experimental import pallas as pl
from jax.experimental.pallas import tpu as pltpu
from jax.sharding import PartitionSpec as P

MESH = pl.DeviceIdType.MESH
F32, BF16 = jnp.float32, jnp.bfloat16

NX, NZ, NL = 4, 8, 4
BL = 28
W = 2 * BL
ROWS = 2 * W
PADDED = 128
HALF = 1280
CHUNK = HALF // 2
SLAB = NZ * 2 * W
PK = 4
TROWS = PK * W
WIN1 = (0, 128, 384, 512)
NT = (((1,), (1,)), ((), ()))
PEERS = 21


def dot(a, b):
    return jnp.dot(a, b, preferred_element_type=F32)


def one_hot(rows, columns, test):
    r = lax.broadcasted_iota(jnp.int32, (rows, columns), 0)
    c = lax.broadcasted_iota(jnp.int32, (rows, columns), 1)
    return jnp.where(test(r, c), 1.0, 0.0).astype(BF16)


class Ring:
    def __init__(self, n, pos, slot, device, send, recv):
        self.n, self.pos, self.slot, self.device, self.send, self.recv = n, pos, slot, device, send, recv
        self.steps = n - 1

    def copy(self, way, step, back):
        q = step % 2 if way == 0 else 1 - step % 2
        j = step // 2 + back
        block = lax.rem(self.pos + (self.n - j if way == 0 else j), self.n)
        ref = self.slot(q, block)
        to = lax.rem(self.pos + (1 if way == 0 else self.n - 1), self.n)
        return pltpu.make_async_remote_copy(
            src_ref=ref,
            dst_ref=ref,
            send_sem=self.send.at[way, step],
            recv_sem=self.recv.at[way, step],
            device_id=self.device(to),
            device_id_type=MESH,
        )

    def start(self, way, step):
        self.copy(way, step, 0).start()

    def step(self, step):
        for way in (0, 1):
            self.copy(way, step, 1).wait_recv()
            if step + 2 < self.steps:
                self.start(way, step + 2)

    def finish(self):
        for step in range(self.steps):
            for way in (0, 1):
                self.copy(way, step, 0).wait_send()


def kernel(
    f_hbm, t_hbm, out_ref,
    fm, fo, df, tm, to, tf, tb, zb, xh, xo, p1, v2, t1, t2, s1, ex, iscr, tex, acc, red0, red1, red2,
    loc, cs, cr, zs, zr, xs, xr, os, orr, ys, yr, p1s, p1r, p2s, p2r, ls, lr, c1s, c1r, c2s, c2r, rs, rr,
):
    blk = lax.axis_index("blk")
    l = lax.axis_index("aux")
    k = lax.rem(blk, 2)
    h = lax.rem(lax.div(blk, 2), 2)
    z = lax.rem(lax.div(blk, 4), NZ)
    x = lax.div(blk, 4 * NZ)
    m = lax.rem(l, 2)

    def at(x_, z_, h_, k_, l_):
        return (((x_ * NZ + z_) * 2 + h_) * 2 + k_, l_)

    other_core = at(x, z, h, 1 - k, l)
    other_half = at(x, z, 1 - h, k, l)
    partner = at(x, z, h, k, l + 1 - 2 * m)

    def xk_peer(o):
        g = lax.rem(x * 2 + k + o, 8)
        return at(lax.div(g, 2), z, h, lax.rem(g, 2), l)

    def z_peer(o):
        return at(x, lax.rem(z + o, NZ), h, k, l)

    def y_peer(o):
        g = lax.rem(h * NL + l + o, 8)
        return at(x, z, lax.div(g, NL), k, lax.rem(g, NL))

    def remote(src, dst, send, recv, device):
        return pltpu.make_async_remote_copy(
            src_ref=src, dst_ref=dst, send_sem=send, recv_sem=recv, device_id=device, device_id_type=MESH
        )

    own_q = pl.multiple_of(k * HALF, 128)
    other_q = pl.multiple_of((1 - k) * HALF, 128)
    load_f = pltpu.make_async_copy(f_hbm.at[:, :, pl.ds(own_q, HALF)], fm, loc.at[0])
    load_t = pltpu.make_async_copy(t_hbm.at[pl.ds(PK * k, PK)], tm, loc.at[1])
    load_f.start()
    load_t.start()

    barrier = pltpu.get_barrier_semaphore()
    for o in range(1, 8):
        for peer in (xk_peer(o), z_peer(o), y_peer(o)):
            pl.semaphore_signal(barrier, inc=1, device_id=peer, device_id_type=MESH)

    zero = jnp.zeros((PADDED - ROWS, CHUNK), BF16)
    for q in range(2):
        for i in range(NZ):
            zb[q, i, pl.ds(ROWS, PADDED - ROWS), :] = zero
        for i in range(NX):
            xo[q, i, pl.ds(ROWS, PADDED - ROWS), :] = zero
    acc[...] = jnp.zeros_like(acc)
    for i in range(4):
        s1[i] = one_hot(
            384, 128, lambda r, c: ((c % 64) < W) & (r == (2 * i + c // 64) * 2 * W + h * W + c % 64 - WIN1[i])
        )
    for i in range(2):
        ex[i] = one_hot(
            128, 128, lambda r, c: (c < 2 * W) & (r == 64 * i + jnp.where(c < W, c, c - W))
        )

    pl.semaphore_wait(barrier, PEERS)

    swap_f = remote(f_hbm.at[:, :, pl.ds(other_q, HALF)], fo, cs.at[0], cr.at[0], other_core)
    swap_t = remote(t_hbm.at[pl.ds(PK * (1 - k), PK)], to, cs.at[1], cr.at[1], other_core)
    swap_f.start()
    swap_t.start()

    load_f.wait()
    swap_f.wait_recv()
    for a in range(2):
        for kk in range(2):
            df[pl.ds(a * W + kk * BL, BL), :] = jnp.where(k == kk, fm[a].astype(F32), fo[a].astype(F32))
    for q in range(2):
        chunk = df[:, q * CHUNK : (q + 1) * CHUNK].astype(BF16)
        zb[q, z, pl.ds(0, ROWS), :] = chunk
        xh[q, x] = chunk

    ring_z = Ring(NZ, z, lambda q, i: zb.at[q, i, pl.ds(0, ROWS)], lambda i: at(x, i, h, k, l), zs, zr)
    ring_x = Ring(NX, x, lambda q, i: xh.at[q, i], lambda i: at(i, z, h, k, l), xs, xr)
    ring_o = Ring(NX, x, lambda q, i: xo.at[q, i, pl.ds(0, ROWS)], lambda i: at(i, z, h, k, l), os, orr)

    def swap_y(q):
        return remote(xh.at[q, x], xo.at[q, x, pl.ds(0, ROWS)], ys.at[q], yr.at[q], other_half)

    for step in range(2):
        for way in (0, 1):
            ring_z.start(way, step)
        for way in (0, 1):
            ring_x.start(way, step)
        swap_y(step).start()

    load_t.wait()
    swap_t.wait_recv()
    for s in range(NX):
        for p in range(PK):
            for kk in range(2):
                mine = tm[p, :, s * SLAB : (s + 1) * SLAB].astype(F32)
                theirs = to[p, :, s * SLAB : (s + 1) * SLAB].astype(F32)
                tf[pl.ds(p * W + kk * BL, BL), :] = jnp.where(k == kk, mine, theirs)
        tb[s] = tf[...].astype(BF16)

    def send_p1(o):
        to_x = lax.rem(x + o, NX)
        return remote(p1.at[to_x], t1.at[k, x], p1s.at[o], p1r.at[o], at(to_x, z, h, k, l))

    def send_p2(o):
        to_z = lax.rem(z + o, NZ)
        return remote(v2.at[to_z], t2.at[k, z, m], p2s.at[o], p2r.at[o], at(x, to_z, h, k, l))

    for s in range(NX):
        for i in range(4):
            p1[s, i] = dot(tb[s, :, WIN1[i] : WIN1[i] + 384], s1[i]).astype(BF16)
    for o in range(1, NX):
        send_p1(o).start()
    for i in range(NZ):
        first = min(128 * (i * 2 * W // 128), SLAB - 256)
        base = i * 2 * W - first
        low = one_hot(256, 128, lambda r, c: (c < W) & (r == base + (1 - h) * W + c))
        high = one_hot(256, 128, lambda r, c: (c >= 64) & (c < 64 + W) & (r == base + (1 - h) * W + c - 64))
        v2[i] = (
            dot(tb[2 * m, :, first : first + 256], low) + dot(tb[2 * m + 1, :, first : first + 256], high)
        ).astype(BF16)
    for o in range(1, NZ):
        send_p2(o).start()
    t1[k, x] = p1[x]
    t2[k, z, m] = v2[z]

    def t1_forward(o):
        ref = t1.at[k, lax.rem(x + NX - o, NX)]
        return remote(ref, ref, c1s.at[o], c1r.at[o], other_core)

    def t1_arrived(o):
        ref = t1.at[1 - k, lax.rem(x + NX - o, NX)]
        return remote(ref, ref, c1s.at[o], c1r.at[o], other_core)

    def p1_arrived(o):
        ref = t1.at[k, lax.rem(x + NX - o, NX)]
        return remote(ref, ref, p1s.at[o], p1r.at[o], other_core)

    def p2_arrived(o):
        ref = t2.at[k, lax.rem(z + NZ - o, NZ), m]
        return remote(ref, ref, p2s.at[o], p2r.at[o], other_core)

    def t2_share(o):
        ref = t2.at[k, lax.rem(z + NZ - o, NZ), m]
        return remote(ref, ref, ls.at[o], lr.at[o], partner)

    def share_arrived(o):
        ref = t2.at[k, lax.rem(z + NZ - o, NZ), 1 - m]
        return remote(ref, ref, ls.at[o], lr.at[o], partner)

    def t2_forward(o, part):
        ref = t2.at[k, lax.rem(z + NZ - o, NZ), m if part == 0 else 1 - m]
        return remote(ref, ref, c2s.at[part, o], c2r.at[part, o], other_core)

    def t2_arrived(o, part):
        ref = t2.at[1 - k, lax.rem(z + NZ - o, NZ), m if part == 0 else 1 - m]
        return remote(ref, ref, c2s.at[part, o], c2r.at[part, o], other_core)

    t1_forward(0).start()
    t2_share(0).start()
    t2_forward(0, 0).start()

    def multiply(block, tiles, which):
        spread = ex[which]
        for kk in range(2):
            tex[pl.ds(kk * TROWS, TROWS), :] = dot(tiles(kk), spread)
        i0 = iscr[pl.ds(pl.multiple_of(block * ROWS, 8), W), :]
        i1 = iscr[pl.ds(pl.multiple_of(block * ROWS + W, 8), W), :]
        for p in range(2 * PK):
            t = tex[pl.ds(p * W, W), :]
            acc[2 * p] += jnp.sum((i0 * t).reshape(W // 8, 8, 128), axis=0)
            acc[2 * p + 1] += jnp.sum((i1 * t).reshape(W // 8, 8, 128), axis=0)

    def own_half(o):
        zi = lax.rem(z + o, NZ)
        total = 0.0
        for q in range(2):
            total += lax.dot_general(
                xh[q].reshape(NX * ROWS, CHUNK), zb[q, zi], NT, preferred_element_type=F32
            )
        iscr[...] = total

        def body(b, _):
            multiply(b, lambda kk: t1[kk, b, lax.div(zi, 2)], lax.rem(zi, 2))
            return 0

        lax.fori_loop(0, NX, body, 0)

    def cross_half(offsets):
        zis = [lax.rem(z + o, NZ) for o in offsets]

        def body(b, _):
            total = 0.0
            for q in range(2):
                rows = jnp.concatenate([zb[q, zi, pl.ds(0, ROWS), :] for zi in zis], axis=0)
                total += lax.dot_general(rows, xo[q, b], NT, preferred_element_type=F32)
            iscr[...] = total
            for i, zi in enumerate(zis):
                multiply(i, lambda kk: t2[kk, zi, lax.div(b, 2)], lax.rem(b, 2))
            return 0

        lax.fori_loop(0, NX, body, 0)

    ring_z.step(0)
    ring_x.step(0)
    ring_z.step(1)
    ring_x.step(1)
    ring_z.step(2)
    ring_x.step(2)
    swap_y(0).wait_recv()
    ring_o.start(0, 0)
    ring_o.start(1, 1)
    ring_z.step(3)
    swap_y(1).wait_recv()
    ring_o.start(0, 1)
    ring_o.start(1, 0)
    for o in range(1, NX):
        p1_arrived(o).wait_recv()
        t1_forward(o).start()
    ring_z.step(4)
    ring_o.step(0)
    for o in range(NX):
        t1_arrived(o).wait_recv()
    own_half(0)
    ring_z.step(5)
    ring_o.step(1)
    for o in (1, 7):
        own_half(o)
    ring_z.step(6)
    ring_o.step(2)

    def pass_on(o, _):
        p2_arrived(o).wait_recv()
        t2_share(o).start()
        t2_forward(o, 0).start()
        return 0

    lax.fori_loop(1, NZ, pass_on, 0)
    for o in (2, 6, 3, 5, 4):
        own_half(o)

    def pass_shared(o, _):
        share_arrived(o).wait_recv()
        t2_forward(o, 1).start()
        return 0

    lax.fori_loop(0, NZ, pass_shared, 0)

    def settle(o, _):
        t2_arrived(o, 0).wait_recv()
        t2_arrived(o, 1).wait_recv()
        return 0

    lax.fori_loop(0, NZ, settle, 0)
    cross_half((0, 1, 7, 2))
    cross_half((6, 3, 5, 4))

    total = jnp.sum(acc[...], axis=1)
    for i, (held, me, peer) in enumerate(
        ((red0, x * 2 + k, xk_peer), (red1, z, z_peer), (red2, h * NL + l, y_peer))
    ):
        held[me] = total
        for o in range(1, 8):
            remote(held.at[me], held.at[me], rs.at[i, o], rr.at[i, o], peer(o)).start()
        for o in range(1, 8):
            ref = held.at[lax.rem(me + 8 - o, 8)]
            remote(ref, ref, rs.at[i, o], rr.at[i, o], peer(o)).wait_recv()
        total = held[0]
        for o in range(1, 8):
            total = total + held[o]
    lane = lax.broadcasted_iota(jnp.int32, total.shape, 1)
    b0 = jnp.sum(jnp.where(lane < W, total, 0.0), axis=1, keepdims=True)
    b1 = jnp.sum(jnp.where(lane < W, 0.0, total), axis=1, keepdims=True)
    both = jnp.where(lax.broadcasted_iota(jnp.int32, (16, 2), 1) == 0, b0, b1)
    for p in range(2 * PK):
        out_ref[p] = both[2 * p : 2 * p + 2, :]

    swap_f.wait_send()
    swap_t.wait_send()
    ring_z.finish()
    ring_x.finish()
    ring_o.finish()
    for q in range(2):
        swap_y(q).wait_send()
    for o in range(1, NX):
        send_p1(o).wait_send()
    for o in range(NX):
        t1_forward(o).wait_send()
    for o in range(1, NZ):
        send_p2(o).wait_send()
    for o in range(NZ):
        t2_share(o).wait_send()
        t2_forward(o, 0).wait_send()
        t2_forward(o, 1).wait_send()
    for i, (held, me, peer) in enumerate(
        ((red0, x * 2 + k, xk_peer), (red1, z, z_peer), (red2, h * NL + l, y_peer))
    ):
        for o in range(1, 8):
            remote(held.at[me], held.at[me], rs.at[i, o], rr.at[i, o], peer(o)).wait_send()


def shards(factors, amplitudes):
    dma = pltpu.SemaphoreType.DMA
    return pl.pallas_call(
        kernel,
        out_shape=jax.ShapeDtypeStruct((2 * PK, 2, 2), F32),
        in_specs=[pl.BlockSpec(memory_space=pl.ANY)] * 2,
        out_specs=pl.BlockSpec(memory_space=pltpu.VMEM),
        scratch_shapes=[
            pltpu.VMEM((2, BL, HALF), BF16),
            pltpu.VMEM((2, BL, HALF), BF16),
            pltpu.VMEM((ROWS, HALF), F32),
            pltpu.VMEM((PK, BL, NX * SLAB), BF16),
            pltpu.VMEM((PK, BL, NX * SLAB), BF16),
            pltpu.VMEM((TROWS, SLAB), F32),
            pltpu.VMEM((NX, TROWS, SLAB), BF16),
            pltpu.VMEM((2, NZ, PADDED, CHUNK), BF16),
            pltpu.VMEM((2, NX, ROWS, CHUNK), BF16),
            pltpu.VMEM((2, NX, PADDED, CHUNK), BF16),
            pltpu.VMEM((NX, 4, TROWS, 128), BF16),
            pltpu.VMEM((NZ, TROWS, 128), BF16),
            pltpu.VMEM((2, NX, 4, TROWS, 128), BF16),
            pltpu.VMEM((2, NZ, 2, TROWS, 128), BF16),
            pltpu.VMEM((4, 384, 128), BF16),
            pltpu.VMEM((2, 128, 128), BF16),
            pltpu.VMEM((4 * ROWS, 128), F32),
            pltpu.VMEM((2 * TROWS, 128), F32),
            pltpu.VMEM((16, 8, 128), F32),
            pltpu.VMEM((8, 16, 128), F32),
            pltpu.VMEM((8, 16, 128), F32),
            pltpu.VMEM((8, 16, 128), F32),
            dma((2,)),
            dma((2,)), dma((2,)),
            dma((2, NZ - 1)), dma((2, NZ - 1)),
            dma((2, NX - 1)), dma((2, NX - 1)),
            dma((2, NX - 1)), dma((2, NX - 1)),
            dma((2,)), dma((2,)),
            dma((NX,)), dma((NX,)),
            dma((NZ,)), dma((NZ,)),
            dma((NZ,)), dma((NZ,)),
            dma((NX,)), dma((NX,)),
            dma((2, NZ)), dma((2, NZ)),
            dma((3, 8)), dma((3, 8)),
        ],
        compiler_params=pltpu.CompilerParams(
            collective_id=0, has_side_effects=True, vmem_limit_bytes=48 * 1024 * 1024
        ),
        cost_estimate=pl.CostEstimate(flops=2_500_000_000, bytes_accessed=20_000_000, transcendentals=0),
    )(factors, amplitudes)


def solution(mesh):
    return jax.shard_map(
        shards,
        mesh=mesh,
        in_specs=(P(None, "blk", "aux"), P(None, "blk", None)),
        out_specs=P(),
        check_vma=False,
    )
```

time: 774 us -> 85 us (0.11)
  the two profiles are of different devices: /device:TPU:27 before, /device:TPU:8 now
where the time goes in v1:
time: 85 us; the launch traced here: 84.8 us
  Pallas kernels  81.2 us (96%)
  local copies, waits for them, and re-layouts  3.56 us (4%)
    pallas_call x1, Pallas kernels, shards(): pl.pallas_call(kernel, out_shape=jax.ShapeDtypeStruct((2 * PK, 2, 2), F32...  81.2 us
    unnamed x2, local copies, waits for them, and re-layouts  2.9 us

profile of v1, /device:TPU:8, one launch (start us, length us, event | category | flops | bytes accessed | tf_op | source)
XLA Modules:
  0.0 84.8 jit_solution(3788901455620221547)
XLA Ops:
  0.0 1.0 %copy.3.f_hbm = bf16[2,28,2560]{2,1,0:T(8,128)(2,1)S(1)} copy(bf16[2,28,2560]{2,0,1:T(2,128)(2,1)} %param.2) | data formatting | bytes 573440 | tf_op args[0]
  1.0 1.9 %copy.4.t_hbm = bf16[8,28,3584]{2,1,0:T(8,128)(2,1)S(1)} copy(bf16[8,28,3584]{2,0,1:T(8,128)(2,1)} %param.3) | data formatting | bytes 3211264 | tf_op args[1]
  2.9 81.2 %shard_map.28 = f32[8,2,2]{2,1,0:T(2,128)S(1)} custom-call(bf16[2,28,2560]{2,1,0:T(8,128)(2,1)S(1)} %copy.3.f_hbm, bf16[8,28,3584]{2,1,0:T(8,128)(2,1)S(1)} %copy.4.t_hbm), custom_call_target="tpu_custom_call" | custom-call | flops 2500000000 | bytes 20000000 | tf_op jit(solution)/shard_map/pallas_call | solution.py:379
  84.2 0.7 copy.5

commit v2 on v1

v2 whole, which is shorter than its diff:
```python
import jax
import jax.numpy as jnp
from jax import lax
from jax.experimental import pallas as pl
from jax.experimental.pallas import tpu as pltpu
from jax.sharding import PartitionSpec as P

MESH = pl.DeviceIdType.MESH
F32, BF16 = jnp.float32, jnp.bfloat16

NX, NZ, NL = 4, 8, 4
PAIRS = 8
BL = 28
W = 2 * BL
ROWS = 2 * W
TOP = ROWS - 64
HALF = 1280
CHUNK = HALF // 2
SLAB = NZ * 2 * W
TROWS = BL * PAIRS
WIN1 = (0, 128, 384, 512)
NT = (((1,), (1,)), ((), ()))
PEERS = 21
DEEP = 2


def dot(a, b):
    return jnp.dot(a, b, preferred_element_type=F32)


def one_hot(rows, columns, test):
    r = lax.broadcasted_iota(jnp.int32, (rows, columns), 0)
    c = lax.broadcasted_iota(jnp.int32, (rows, columns), 1)
    return jnp.where(test(r, c), 1.0, 0.0).astype(BF16)


class Ring:
    def __init__(self, n, pos, slot, device, send, recv):
        self.n, self.pos, self.slot, self.device, self.send, self.recv = n, pos, slot, device, send, recv
        self.steps = n - 1

    def copy(self, way, step, back):
        q = step % 2 if way == 0 else 1 - step % 2
        j = step // 2 + back
        block = lax.rem(self.pos + (self.n - j if way == 0 else j), self.n)
        ref = self.slot(q, block)
        to = lax.rem(self.pos + (1 if way == 0 else self.n - 1), self.n)
        return pltpu.make_async_remote_copy(
            src_ref=ref,
            dst_ref=ref,
            send_sem=self.send.at[way, step],
            recv_sem=self.recv.at[way, step],
            device_id=self.device(to),
            device_id_type=MESH,
        )

    def start(self, way, step):
        self.copy(way, step, 0).start()

    def step(self, step):
        for way in (0, 1):
            self.copy(way, step, 1).wait_recv()
            if step + 2 < self.steps:
                self.start(way, step + 2)

    def finish(self):
        for step in range(self.steps):
            for way in (0, 1):
                self.copy(way, step, 0).wait_send()


def kernel(
    f_hbm, t_hbm, out_ref,
    fm, fo, df, tm, zb, xh, xo, p1, v2, t1, t2, iscr, acc, red0, red1, red2,
    loc, cs, cr, zs, zr, xs, xr, os, orr, ys, yr, p1s, p1r, p2s, p2r, ls, lr, c1s, c1r, c2s, c2r, rs, rr,
):
    blk = lax.axis_index("blk")
    l = lax.axis_index("aux")
    k = lax.rem(blk, 2)
    h = lax.rem(lax.div(blk, 2), 2)
    z = lax.rem(lax.div(blk, 4), NZ)
    x = lax.div(blk, 4 * NZ)
    m = lax.rem(l, 2)

    def at(x_, z_, h_, k_, l_):
        return (((x_ * NZ + z_) * 2 + h_) * 2 + k_, l_)

    other_core = at(x, z, h, 1 - k, l)
    other_half = at(x, z, 1 - h, k, l)
    partner = at(x, z, h, k, l + 1 - 2 * m)

    def xk_peer(o):
        g = lax.rem(x * 2 + k + o, 8)
        return at(lax.div(g, 2), z, h, lax.rem(g, 2), l)

    def z_peer(o):
        return at(x, lax.rem(z + o, NZ), h, k, l)

    def y_peer(o):
        g = lax.rem(h * NL + l + o, 8)
        return at(x, z, lax.div(g, NL), k, lax.rem(g, NL))

    def remote(src, dst, send, recv, device):
        return pltpu.make_async_remote_copy(
            src_ref=src, dst_ref=dst, send_sem=send, recv_sem=recv, device_id=device, device_id_type=MESH
        )

    own_q = pl.multiple_of(k * HALF, 128)
    other_q = pl.multiple_of((1 - k) * HALF, 128)
    load_t = pltpu.make_async_copy(t_hbm, tm, loc.at[1])
    load_f = pltpu.make_async_copy(f_hbm.at[:, :, pl.ds(own_q, HALF)], fm, loc.at[0])
    load_t.start()
    load_f.start()

    barrier = pltpu.get_barrier_semaphore()
    for o in range(1, 8):
        for peer in (xk_peer(o), z_peer(o), y_peer(o)):
            pl.semaphore_signal(barrier, inc=1, device_id=peer, device_id_type=MESH)

    load_t.wait()
    for i in range(4):
        pick = one_hot(
            384, 128, lambda r, c: ((c % 64) < W) & (r == (2 * i + c // 64) * 2 * W + h * W + c % 64 - WIN1[i])
        )
        for s in range(NX):
            first = s * SLAB + WIN1[i]
            p1[s, i] = dot(tm[:, first : first + 384], pick).astype(BF16)
    for i in range(NZ):
        first = min(128 * (i * 2 * W // 128), SLAB - 256)
        base = i * 2 * W - first
        low = one_hot(256, 128, lambda r, c: (c < W) & (r == base + (1 - h) * W + c))
        high = one_hot(256, 128, lambda r, c: (c >= 64) & (c < 64 + W) & (r == base + (1 - h) * W + c - 64))
        low_at = pl.multiple_of(2 * m * SLAB + first, 128)
        high_at = pl.multiple_of((2 * m + 1) * SLAB + first, 128)
        v2[i] = (dot(tm[:, pl.ds(low_at, 256)], low) + dot(tm[:, pl.ds(high_at, 256)], high)).astype(BF16)
    t1[k, x] = p1[x]
    t2[k, z, m] = v2[z]

    acc[...] = jnp.zeros_like(acc)
    load_f.wait()
    for i in range(BL):
        row = fm[i].astype(F32)
        for a in range(2):
            df[pl.ds(a * W + k * BL + i, 1), :] = row[a : a + 1, :]

    pl.semaphore_wait(barrier, PEERS)

    swap_f = remote(f_hbm.at[:, :, pl.ds(other_q, HALF)], fo, cs.at[0], cr.at[0], other_core)
    swap_f.start()

    def send_p1(o):
        to_x = lax.rem(x + o, NX)
        return remote(p1.at[to_x], t1.at[k, x], p1s.at[o], p1r.at[o], at(to_x, z, h, k, l))

    def send_p2(o):
        to_z = lax.rem(z + o, NZ)
        return remote(v2.at[to_z], t2.at[k, z, m], p2s.at[o], p2r.at[o], at(x, to_z, h, k, l))

    def t1_forward(o):
        ref = t1.at[k, lax.rem(x + NX - o, NX)]
        return remote(ref, ref, c1s.at[o], c1r.at[o], other_core)

    def t1_arrived(o):
        ref = t1.at[1 - k, lax.rem(x + NX - o, NX)]
        return remote(ref, ref, c1s.at[o], c1r.at[o], other_core)

    def p1_arrived(o):
        ref = t1.at[k, lax.rem(x + NX - o, NX)]
        return remote(ref, ref, p1s.at[o], p1r.at[o], other_core)

    def p2_arrived(o):
        ref = t2.at[k, lax.rem(z + NZ - o, NZ), m]
        return remote(ref, ref, p2s.at[o], p2r.at[o], other_core)

    def t2_share(o):
        ref = t2.at[k, lax.rem(z + NZ - o, NZ), m]
        return remote(ref, ref, ls.at[o], lr.at[o], partner)

    def share_arrived(o):
        ref = t2.at[k, lax.rem(z + NZ - o, NZ), 1 - m]
        return remote(ref, ref, ls.at[o], lr.at[o], partner)

    def t2_forward(o, part):
        ref = t2.at[k, lax.rem(z + NZ - o, NZ), m if part == 0 else 1 - m]
        return remote(ref, ref, c2s.at[part, o], c2r.at[part, o], other_core)

    def t2_arrived(o, part):
        ref = t2.at[1 - k, lax.rem(z + NZ - o, NZ), m if part == 0 else 1 - m]
        return remote(ref, ref, c2s.at[part, o], c2r.at[part, o], other_core)

    ring_z = Ring(NZ, z, lambda q, i: zb.at[q, i], lambda i: at(x, i, h, k, l), zs, zr)
    ring_x = Ring(NX, x, lambda q, i: xh.at[q, i], lambda i: at(i, z, h, k, l), xs, xr)
    ring_o = Ring(NX, x, lambda q, i: xo.at[q, i], lambda i: at(i, z, h, k, l), os, orr)

    def swap_y(q):
        return remote(xh.at[q, x], xo.at[q, x], ys.at[q], yr.at[q], other_half)

    swap_f.wait_recv()
    for i in range(BL):
        row = fo[i].astype(F32)
        for a in range(2):
            df[pl.ds(a * W + (1 - k) * BL + i, 1), :] = row[a : a + 1, :]
    for q in range(2):
        chunk = df[:, q * CHUNK : (q + 1) * CHUNK].astype(BF16)
        zb[q, z] = chunk
        xh[q, x] = chunk
    for step in range(2):
        for way in (0, 1):
            ring_z.start(way, step)
        for way in (0, 1):
            ring_x.start(way, step)
        swap_y(step).start()

    for o in range(1, NX):
        send_p1(o).start()
    for o in range(1, NZ):
        send_p2(o).start()
    t1_forward(0).start()
    t2_share(0).start()
    t2_forward(0, 0).start()

    def both(buf, q, pair):
        rows = [buf[q, 2 * pair + i, pl.ds(first, 64), :] for first in (0, TOP) for i in range(2)]
        return jnp.concatenate(rows, axis=0)

    def multiply(block, tiles, sums):
        parts = [[None] * 8 for _ in range(4)]
        for kk in range(2):
            low = tiles(kk).astype(F32)
            high = pltpu.roll(low, 8, 1)
            for i in range(BL):
                for a in range(2):
                    row = block * ROWS + a * W + kk * BL + i
                    for b, t in enumerate((low, high)):
                        term = iscr[b, pl.ds(row, 1), :] * t[PAIRS * i : PAIRS * (i + 1), :]
                        held, j = parts[2 * a + b], i % DEEP
                        held[j] = term if held[j] is None else held[j] + term
        return tuple(sums[n] + sum(parts[n][1:DEEP], parts[n][0]) for n in range(4))

    def add_up(work):
        sums = work(tuple(acc[n] for n in range(4)))
        for n in range(4):
            acc[n] = sums[n]

    def keep(integrals):
        for b in range(2):
            iscr[b] = integrals[:, 128 * b : 128 * (b + 1)]

    def own_half(pair):
        pair = lax.rem(pair, NZ // 2)
        total = 0.0
        for q in range(2):
            total += lax.dot_general(
                xh[q].reshape(NX * ROWS, CHUNK), both(zb, q, pair), NT, preferred_element_type=F32
            )
        keep(total)

        def body(b, sums):
            return multiply(b, lambda kk: t1[kk, b, pair], sums)

        add_up(lambda sums: lax.fori_loop(0, NX, body, sums))

    def cross_half(offsets):
        zis = [lax.rem(z + o, NZ) for o in offsets]

        def body(pair, sums):
            total = 0.0
            for q in range(2):
                rows = jnp.concatenate([zb[q, zi] for zi in zis], axis=0)
                total += lax.dot_general(rows, both(xo, q, pair), NT, preferred_element_type=F32)
            keep(total)
            for i, zi in enumerate(zis):
                sums = multiply(i, lambda kk: t2[kk, zi, pair], sums)
            return sums

        add_up(lambda sums: lax.fori_loop(0, NX // 2, body, sums))

    here = lax.div(z, 2)
    turn = 1 - 2 * lax.rem(z, 2)

    def pass_x():
        for o in range(1, NX):
            p1_arrived(o).wait_recv()
            t1_forward(o).start()

    def pass_z():
        def pass_on(o, _):
            p2_arrived(o).wait_recv()
            t2_share(o).start()
            t2_forward(o, 0).start()
            return 0

        lax.fori_loop(1, NZ, pass_on, 0)

    def pass_shared():
        def pass_on(o, _):
            share_arrived(o).wait_recv()
            t2_forward(o, 1).start()
            return 0

        lax.fori_loop(0, NZ, pass_on, 0)

    def settle_x():
        for o in range(NX):
            t1_arrived(o).wait_recv()

    def settle_z():
        def settle(o, _):
            t2_arrived(o, 0).wait_recv()
            t2_arrived(o, 1).wait_recv()
            return 0

        lax.fori_loop(0, NZ, settle, 0)

    def swapped(q):
        swap_y(q).wait_recv()
        ring_o.start(0, q)
        ring_o.start(1, 1 - q)

    ring_z.step(0)
    ring_x.step(0)
    ring_z.step(1)
    ring_x.step(1)
    ring_x.step(2)
    ring_z.step(2)
    swapped(0)
    pass_x()
    ring_z.step(3)
    swapped(1)
    settle_x()
    own_half(here)
    pass_z()
    ring_z.step(4)
    ring_o.step(0)
    own_half(here + 4 - turn)
    pass_shared()
    ring_z.step(5)
    ring_o.step(1)
    own_half(here + 4 + turn)
    settle_z()
    ring_o.step(2)
    cross_half((0, 1, 7, 2))
    ring_z.step(6)
    own_half(here + 2)
    cross_half((6, 3, 5, 4))

    lane = lax.broadcasted_iota(jnp.int32, (PAIRS, 128), 1)
    total = jnp.zeros((PAIRS, 128), F32)
    for n in range(4):
        total = jnp.where(lane == n, jnp.sum(acc[n], axis=1, keepdims=True), total)
    rounds = ((red0, x * 2 + k, xk_peer), (red1, z, z_peer), (red2, h * NL + l, y_peer))
    for i, (held, me, peer) in enumerate(rounds):
        held[me] = total
        for o in range(1, 8):
            remote(held.at[me], held.at[me], rs.at[i, o], rr.at[i, o], peer(o)).start()
        for o in range(1, 8):
            ref = held.at[lax.rem(me + 8 - o, 8)]
            remote(ref, ref, rs.at[i, o], rr.at[i, o], peer(o)).wait_recv()
        total = held[0]
        for o in range(1, 8):
            total = total + held[o]
    diagonal = lax.broadcasted_iota(jnp.int32, (PAIRS, PAIRS), 0) == lax.broadcasted_iota(
        jnp.int32, (PAIRS, PAIRS), 1
    )
    for a in range(2):
        for b in range(2):
            column = total[:, 2 * a + b : 2 * a + b + 1]
            out_ref[a, pl.ds(b, 1), :] = jnp.sum(jnp.where(diagonal, column, 0.0), axis=0, keepdims=True)

    swap_f.wait_send()
    ring_z.finish()
    ring_x.finish()
    ring_o.finish()
    for q in range(2):
        swap_y(q).wait_send()
    for o in range(1, NX):
        send_p1(o).wait_send()
    for o in range(NX):
        t1_forward(o).wait_send()
    for o in range(1, NZ):
        send_p2(o).wait_send()
    for o in range(NZ):
        t2_share(o).wait_send()
        t2_forward(o, 0).wait_send()
        t2_forward(o, 1).wait_send()
    for i, (held, me, peer) in enumerate(rounds):
        for o in range(1, 8):
            remote(held.at[me], held.at[me], rs.at[i, o], rr.at[i, o], peer(o)).wait_send()


def shards(factors, amplitudes):
    dma = pltpu.SemaphoreType.DMA
    by_orbital = jnp.transpose(amplitudes, (1, 0, 2)).reshape(TROWS, NX * SLAB)
    out = pl.pallas_call(
        kernel,
        out_shape=jax.ShapeDtypeStruct((2, 2, PAIRS), F32),
        in_specs=[pl.BlockSpec(memory_space=pl.ANY)] * 2,
        out_specs=pl.BlockSpec(memory_space=pltpu.VMEM),
        scratch_shapes=[
            pltpu.VMEM((BL, 2, HALF), BF16),
            pltpu.VMEM((BL, 2, HALF), BF16),
            pltpu.VMEM((ROWS, HALF), F32),
            pltpu.VMEM((TROWS, NX * SLAB), BF16),
            pltpu.VMEM((2, NZ, ROWS, CHUNK), BF16),
            pltpu.VMEM((2, NX, ROWS, CHUNK), BF16),
            pltpu.VMEM((2, NX, ROWS, CHUNK), BF16),
            pltpu.VMEM((NX, 4, TROWS, 128), BF16),
            pltpu.VMEM((NZ, TROWS, 128), BF16),
            pltpu.VMEM((2, NX, 4, TROWS, 128), BF16),
            pltpu.VMEM((2, NZ, 2, TROWS, 128), BF16),
            pltpu.VMEM((2, 4 * ROWS, 128), F32),
            pltpu.VMEM((4, PAIRS, 128), F32),
            pltpu.VMEM((8, PAIRS, 128), F32),
            pltpu.VMEM((8, PAIRS, 128), F32),
            pltpu.VMEM((8, PAIRS, 128), F32),
            dma((2,)),
            dma((2,)), dma((2,)),
            dma((2, NZ - 1)), dma((2, NZ - 1)),
            dma((2, NX - 1)), dma((2, NX - 1)),
            dma((2, NX - 1)), dma((2, NX - 1)),
            dma((2,)), dma((2,)),
            dma((NX,)), dma((NX,)),
            dma((NZ,)), dma((NZ,)),
            dma((NZ,)), dma((NZ,)),
            dma((NX,)), dma((NX,)),
            dma((2, NZ)), dma((2, NZ)),
            dma((3, 8)), dma((3, 8)),
        ],
        compiler_params=pltpu.CompilerParams(
            collective_id=0, has_side_effects=True, vmem_limit_bytes=62 * 1024 * 1024
        ),
        cost_estimate=pl.CostEstimate(flops=2_500_000_000, bytes_accessed=20_000_000, transcendentals=0),
    )(jnp.transpose(factors, (1, 0, 2)), by_orbital)
    return jnp.transpose(out, (2, 0, 1))


def solution(mesh):
    return jax.shard_map(
        shards,
        mesh=mesh,
        in_specs=(P(None, "blk", "aux"), P(None, "blk", None)),
        out_specs=P(),
        check_vma=False,
    )
```

time: 85 us -> 75.2 us (0.88)
  Pallas kernels: 81.2 us -> 73.8 us
  local copies, waits for them, and re-layouts: 3.56 us -> 1.26 us
    pallas_call x1, Pallas kernels: 81.2 us -> 73.8 us  [shards(): pl.pallas_call(kernel, out_shape=jax.ShapeDtypeStruct((2, 2, PAIRS), F32)...]
    unnamed x2 -> x1, local copies, waits for them, and re-layouts: 2.9 us -> 1.26 us
where the time goes in v2:
time: 75.2 us; the launch traced here: 75.1 us
  Pallas kernels  73.8 us (98%)
  local copies, waits for them, and re-layouts  1.26 us (2%)
    pallas_call x1, Pallas kernels, shards(): pl.pallas_call(kernel, out_shape=jax.ShapeDtypeStruct((2, 2, PAIRS), F32)...  73.8 us

profile of v2, /device:TPU:8, one launch (start us, length us, event | category | flops | bytes accessed | tf_op | source)
XLA Modules:
  0.0 75.1 jit_solution(12098472321545186427)
XLA Ops:
  0.0 73.8 %shard_map.28 = f32[2,2,8]{2,1,0:T(2,128)} custom-call(bf16[28,2,2560]{2,1,0:T(2,128)(2,1)} %bitcast.7, bf16[224,3584]{1,0:T(8,128)(2,1)} %bitcast.6), custom_call_target="tpu_custom_call" | custom-call | flops 2500000000 | bytes 20000000 | tf_op jit(solution)/shard_map/pallas_call | solution.py:394
  73.8 1.3 %copy.4 = f32[8,2,2]{0,2,1:T(2,128)} copy(f32[8,2,2]{0,2,1:T(2,128)} %bitcast.5) | data formatting | bytes 256

commit v3 on v2

--- a/solution.py
+++ b/solution.py
@@ -195,6 +195,13 @@
     def swap_y(q):
         return remote(xh.at[q, x], xo.at[q, x], ys.at[q], yr.at[q], other_half)
 
+    for o in range(1, NX):
+        send_p1(o).start()
+    for o in range(1, NZ):
+        send_p2(o).start()
+    t1_forward(0).start()
+    t2_share(0).start()
+    t2_forward(0, 0).start()
     swap_f.wait_recv()
     for i in range(BL):
         row = fo[i].astype(F32)
@@ -211,13 +218,6 @@
             ring_x.start(way, step)
         swap_y(step).start()
 
-    for o in range(1, NX):
-        send_p1(o).start()
-    for o in range(1, NZ):
-        send_p2(o).start()
-    t1_forward(0).start()
-    t2_share(0).start()
-    t2_forward(0, 0).start()
 
     def both(buf, q, pair):
         rows = [buf[q, 2 * pair + i, pl.ds(first, 64), :] for first in (0, TOP) for i in range(2)]
@@ -244,7 +244,7 @@
 
     def keep(integrals):
         for b in range(2):
-            iscr[b] = integrals[:, 128 * b : 128 * (b + 1)]
+            iscr[b, pl.ds(0, integrals.shape[0]), :] = integrals[:, 128 * b : 128 * (b + 1)]
 
     def own_half(pair):
         pair = lax.rem(pair, NZ // 2)
@@ -317,32 +317,33 @@
         ring_o.start(0, q)
         ring_o.start(1, 1 - q)
 
+    ring_x.step(0)
     ring_z.step(0)
-    ring_x.step(0)
+    ring_x.step(1)
     ring_z.step(1)
-    ring_x.step(1)
+    pass_x()
     ring_x.step(2)
+    swapped(0)
     ring_z.step(2)
-    swapped(0)
-    pass_x()
+    pass_z()
+    swapped(1)
     ring_z.step(3)
-    swapped(1)
     settle_x()
     own_half(here)
-    pass_z()
     ring_z.step(4)
     ring_o.step(0)
+    pass_shared()
     own_half(here + 4 - turn)
-    pass_shared()
+    ring_o.step(1)
     ring_z.step(5)
-    ring_o.step(1)
+    settle_z()
     own_half(here + 4 + turn)
-    settle_z()
     ring_o.step(2)
     cross_half((0, 1, 7, 2))
+    cross_half((6, 3, 5))
     ring_z.step(6)
     own_half(here + 2)
-    cross_half((6, 3, 5, 4))
+    cross_half((4,))
 
     lane = lax.broadcasted_iota(jnp.int32, (PAIRS, 128), 1)
     total = jnp.zeros((PAIRS, 128), F32)

time: 75.2 us -> 69.9 us (0.930)
  Pallas kernels: 73.8 us -> 68.4 us
    pallas_call x1, Pallas kernels: 73.8 us -> 68.4 us  [shards(): pl.pallas_call(kernel, out_shape=jax.ShapeDtypeStruct((2, 2, PAIRS), F32)...]
where the time goes in v3:
time: 69.9 us; the launch traced here: 69.7 us
  Pallas kernels  68.4 us (98%)
  local copies, waits for them, and re-layouts  1.26 us (2%)
    pallas_call x1, Pallas kernels, shards(): pl.pallas_call(kernel, out_shape=jax.ShapeDtypeStruct((2, 2, PAIRS), F32)...  68.4 us

profile of v3, /device:TPU:8, one launch (start us, length us, event | category | flops | bytes accessed | tf_op | source)
XLA Modules:
  0.0 69.7 jit_solution(14792578404593116959)
XLA Ops:
  0.0 68.4 %shard_map.28 = f32[2,2,8]{2,1,0:T(2,128)} custom-call(bf16[28,2,2560]{2,1,0:T(2,128)(2,1)} %bitcast.7, bf16[224,3584]{1,0:T(8,128)(2,1)} %bitcast.6), custom_call_target="tpu_custom_call" | custom-call | flops 2500000000 | bytes 20000000 | tf_op jit(solution)/shard_map/pallas_call | solution.py:395
  68.4 1.3 %copy.4 = f32[8,2,2]{0,2,1:T(2,128)} copy(f32[8,2,2]{0,2,1:T(2,128)} %bitcast.5) | data formatting | bytes 256
